TPU v7x, 256 devices: a whole 4x4x8 slice. The times are simulated.
256 devices in a mesh: px: 32 (over x, y, core), py: 8 (over z).
Axes of the slice: x: 4, y: 4, z: 8, core: 2. Of those that a mesh axis runs over, the one named last changes fastest.
Arguments:
- forcing: float32 [3, 224, 56, 7, 128], P(None, 'px', 'py'), may hold values from -600 to 600
- initial_guess: float32 [3, 224, 56, 7, 128], P(None, 'px', 'py'), may hold values from -3 to 3
- forward_velocity: bfloat16 [3, 224, 56, 7, 128], P(None, 'px', 'py'), may hold values from -4 to 4
- free_mask: int32 [224, 56, 7, 128], P('px', 'py'), may hold values 0 or 1
Outputs:
- adjoint_velocity: float32 [3, 224, 56, 7, 128], P(None, 'px', 'py')
- search_direction: float32 [3, 224, 56, 7, 128], P(None, 'px', 'py')
Inputs may be any that keep to these rules, and one draw needn't show every extreme that they name: `free_mask`: 1 marks a free node, 0 a node held at its initial guess.
All inputs are finite; a program needn't handle non-finite values. No bound on the sum of `free_mask` on one device may be relied on, other than what follows from the above.
Results may differ from a plain program's by a relative error of at most 0.00085.
Values sent between devices are 32-bit elements; how exact they have to be, the bound alone decides.
A program may use at most 64 MiB of HBM per device.

v0:
```python
import jax
import jax.numpy as jnp
import numpy as np
from jax import lax
from jax.sharding import PartitionSpec as P

ITERS = 2
VISC_BASE = 0.5
VISC_GAIN = 0.5
HELMHOLTZ = 20.0


def shifted(value, axis, by):
    count = lax.axis_size(axis)
    return lax.ppermute(value, axis, [(i, (i + by) % count) for i in range(count)])


def passed_along(block, axis, distance):
    devices = range(lax.axis_size(axis))
    route = [(i - distance, i) for i in devices if i - distance in devices]
    return lax.ppermute(block, axis, route)


def gll_tables():
    poly_order = 7
    gll_points = np.array(
        [
            -1.0,
            -0.8717401485096066,
            -0.5917001814331423,
            -0.20929921790247888,
            0.20929921790247888,
            0.5917001814331423,
            0.8717401485096066,
            1.0,
        ]
    )
    previous = np.ones(8)
    legendre = gll_points.copy()
    for degree in range(1, poly_order):
        following = ((2 * degree + 1) * gll_points * legendre - degree * previous) / (degree + 1)
        previous = legendre
        legendre = following
    quad_weights = 2.0 / (poly_order * (poly_order + 1) * legendre**2)
    derivative = np.zeros((8, 8))
    for target in range(8):
        for source in range(8):
            if target != source:
                derivative[target, source] = (
                    legendre[target] / legendre[source] / (gll_points[target] - gll_points[source])
                )
    derivative[0, 0] = -poly_order * (poly_order + 1) / 4.0
    derivative[7, 7] = poly_order * (poly_order + 1) / 4.0
    node_weights = quad_weights[:7].copy()
    node_weights[0] = 2.0 * quad_weights[0]
    return (quad_weights, derivative, node_weights)


def line_weights(length):
    node_weights = gll_tables()[2]
    return jnp.asarray(np.tile(node_weights, length // 7), jnp.float32)


def local_view(values, dimension, elements):
    leading = lax.slice_in_dim(values, 0, 7 * elements, axis=dimension)
    leading = leading.reshape(
        values.shape[:dimension] + (elements, 7) + values.shape[dimension + 1 :]
    )
    closing = lax.slice_in_dim(values, 7, 7 * elements + 1, stride=7, axis=dimension)
    closing = jnp.expand_dims(closing, dimension + 1)
    return jnp.concatenate([leading, closing], axis=dimension + 1)


def fold_view(local_part, dimension, elements):
    leading = lax.slice_in_dim(local_part, 0, 7, axis=dimension + 1)
    out_shape = local_part.shape[:dimension] + (7 * elements,) + local_part.shape[dimension + 2 :]
    leading = leading.reshape(out_shape)
    closing = lax.slice_in_dim(local_part, 7, 8, axis=dimension + 1)
    padding = jnp.zeros(
        closing.shape[: dimension + 1] + (6,) + closing.shape[dimension + 2 :], local_part.dtype
    )
    closing = jnp.concatenate([padding, closing], axis=dimension + 1).reshape(out_shape)
    zero_node = jnp.zeros(
        out_shape[:dimension] + (1,) + out_shape[dimension + 1 :], local_part.dtype
    )
    return jnp.concatenate([leading, zero_node], axis=dimension) + jnp.concatenate(
        [zero_node, closing], axis=dimension
    )


def z_view(values):
    first_layer = values[..., 0:1, :]
    return jnp.concatenate([values, jnp.roll(first_layer, -1, axis=-1)], axis=-2)


def z_fold(local_part):
    first_node = local_part[..., 0:1, :] + jnp.roll(local_part[..., 7:8, :], 1, axis=-1)
    return jnp.concatenate([first_node, local_part[..., 1:7, :]], axis=-2)


def kernel(values, coef_part, trailing):
    quad_weights, derivative, node_weights = gll_tables()
    deriv_table = jnp.asarray(derivative, jnp.float32)
    weight_column = jnp.asarray(quad_weights, jnp.float32).reshape((8,) + (1,) * trailing)
    index_tail = "sab"[3 - trailing :]
    gradient = jnp.einsum(
        "mk,...k" + index_tail + "->...m" + index_tail,
        deriv_table,
        values,
        precision=lax.Precision.HIGHEST,
    )
    flux_term = gradient * (weight_column * coef_part)
    return jnp.einsum(
        "mk,...m" + index_tail + "->...k" + index_tail,
        deriv_table,
        flux_term,
        precision=lax.Precision.HIGHEST,
    )


def diag_kernel(coef_part, trailing):
    quad_weights, derivative, node_weights = gll_tables()
    square_table = jnp.asarray(derivative * derivative, jnp.float32)
    weight_column = jnp.asarray(quad_weights, jnp.float32).reshape((8,) + (1,) * trailing)
    index_tail = "sab"[3 - trailing :]
    return jnp.einsum(
        "mk,...m" + index_tail + "->...k" + index_tail,
        square_table,
        weight_column * coef_part,
        precision=lax.Precision.HIGHEST,
    )


def element_factor():
    return 1.0


def direction_term(values, coef_ext, from_right):
    field_dim = values.ndim - from_right
    coef_dim = coef_ext.ndim - from_right
    elements = (values.shape[field_dim] - 1) // 7
    local_part = kernel(
        local_view(values, field_dim, elements),
        local_view(coef_ext, coef_dim, elements),
        from_right - 1,
    )
    local_part = local_part * element_factor()
    return fold_view(local_part, field_dim, elements)


def diag_term(coef_ext, from_right):
    coef_dim = coef_ext.ndim - from_right
    elements = (coef_ext.shape[coef_dim] - 1) // 7
    local_part = diag_kernel(local_view(coef_ext, coef_dim, elements), from_right - 1)
    local_part = local_part * element_factor()
    return fold_view(local_part, coef_dim, elements)


def extend_x(values):
    dimension = values.ndim - 4
    first_layer = lax.slice_in_dim(values, 0, 1, axis=dimension)
    upper_part = shifted(first_layer, "px", -1)
    return jnp.concatenate([values, upper_part], axis=dimension)


def extend_y(values):
    dimension = values.ndim - 3
    first_layer = lax.slice_in_dim(values, 0, 1, axis=dimension)
    upper_part = passed_along(first_layer, "py", -1)
    return jnp.concatenate([values, upper_part], axis=dimension)


def reduce_x(values):
    dimension = values.ndim - 4
    length = values.shape[dimension]
    last_node = lax.slice_in_dim(values, length - 1, length, axis=dimension)
    arrived = shifted(last_node, "px", 1)
    first_node = lax.slice_in_dim(values, 0, 1, axis=dimension) + arrived
    return jnp.concatenate(
        [first_node, lax.slice_in_dim(values, 1, length - 1, axis=dimension)], axis=dimension
    )


def reduce_y(values):
    dimension = values.ndim - 3
    length = values.shape[dimension]
    last_node = lax.slice_in_dim(values, length - 1, length, axis=dimension)
    arrived = passed_along(last_node, "py", 1)
    first_node = lax.slice_in_dim(values, 0, 1, axis=dimension) + arrived
    return jnp.concatenate(
        [first_node, lax.slice_in_dim(values, 1, length - 1, axis=dimension)], axis=dimension
    )


def spread(totals):
    return totals.reshape(3, 1, 1, 1, 1)


def energy_sum(residual, precond):
    return lax.psum(jnp.sum(residual * precond, axis=(1, 2, 3, 4)), ("px", "py"))


def body(forcing, initial_guess, forward_velocity, free_mask):
    free_float = free_mask.astype(jnp.float32)
    speed_sq = jnp.sum(jnp.square(forward_velocity.astype(jnp.float32)), axis=0)
    viscosity = VISC_BASE + VISC_GAIN * speed_sq
    weight_x = line_weights(free_mask.shape[0])[:, None, None, None]
    weight_y = line_weights(free_mask.shape[1])[:, None, None]
    weight_z = line_weights(7)[:, None]
    coef_x = viscosity * weight_y * weight_z
    coef_y = viscosity * weight_x * weight_z
    coef_z = viscosity * weight_x * weight_y
    mass_diag = weight_x * weight_y * weight_z * jnp.ones((free_mask.shape[3],), jnp.float32)
    coef_x_ext = extend_x(coef_x)
    coef_y_ext = extend_y(coef_y)
    diag_x = reduce_x(diag_term(coef_x_ext, 4))
    diag_y = reduce_y(diag_term(coef_y_ext, 3))
    diag_z = z_fold(diag_kernel(z_view(coef_z), 1))
    diagonal = diag_x + diag_y + diag_z + HELMHOLTZ * mass_diag
    coef_z_view = z_view(coef_z)

    def operate(values):
        term_x = reduce_x(direction_term(extend_x(values), coef_x_ext, 4))
        term_y = reduce_y(direction_term(extend_y(values), coef_y_ext, 3))
        term_z = z_fold(kernel(z_view(values), coef_z_view, 1))
        return free_float * (term_x + term_y + term_z + HELMHOLTZ * mass_diag * values)

    right_side = free_float * mass_diag * forcing
    solution = initial_guess
    residual = right_side - operate(initial_guess)
    precond = residual / diagonal
    energy_now = energy_sum(residual, precond)
    direction = precond
    for iteration in range(ITERS):
        applied = operate(direction)
        curvature = lax.psum(jnp.sum(direction * applied, axis=(1, 2, 3, 4)), ("px", "py"))
        step_length = spread(energy_now / curvature)
        solution = solution + step_length * direction
        residual = residual - step_length * applied
        precond = residual / diagonal
        energy_next = energy_sum(residual, precond)
        direction = precond + spread(energy_next / energy_now) * direction
        energy_now = energy_next
    return (solution, direction)


def solution(mesh):
    placed = (
        P(None, "px", "py", None, None),
        P(None, "px", "py", None, None),
        P(None, "px", "py", None, None),
        P("px", "py", None, None),
    )
    return jax.shard_map(
        body,
        mesh=mesh,
        in_specs=placed,
        out_specs=(P(None, "px", "py", None, None), P(None, "px", "py", None, None)),
        check_vma=False,
    )
```

profile of v0, /device:TPU:1, one launch (start us, length us, event | category | flops | bytes accessed | tf_op | source)
XLA Modules:
  0.0 393.7 jit_solution(17573299616021403080)
XLA Ops:
  0.6 1.1 multiply_reduce_fusion.5
  1.9 1.3 collective-permute-start.4
  3.8 3.2 collective-permute-start.1
  7.0 0.7 copy.257
  7.7 2.9 collective-permute-start
  10.6 0.7 copy.258
  11.3 1.3 collective-permute-start.3
  15.7 0.7 fusion.2
  16.4 0.7 fusion.52
  17.6 0.7 copy-done.8
  19.0 0.9 maximum_multiply_fusion
  20.3 4.8 %collective-permute-start.7 = (f32[7,1,7,128]{3,0,2,1:T(8,128)S(1)}, f32[7,1,7,128]{3,0,2,1:T(8,128)S(1)}, u32[]{:S(2)}, u32[]{:S(2)}) collective-permute-start(f32[7,1,7,128]{3,0,2,1:T(8,128)S(1)} %pad_add_fusion.14), channel_id=1, source_target_pairs={{0,1},{1,2},{2,3},{3,4},{4,5},{5,6},{6,7},{8,9},{9,10},{10,11},{11... | collective-permute-start | bytes 75272 | tf_op jit(solution)/shard_map/ppermute | solution.py:21
  25.2 0.8 maximum_multiply_fusion.2
  26.6 1.8 collective-permute-done.6
  28.6 1.6 fusion.4
  30.2 0.7 convolution_bitcast_fusion.10
  31.2 1.5 collective-permute-start.2
  32.8 0.7 fusion.6
  33.6 0.7 fusion.51
  34.5 3.7 collective-permute-start.5
  38.6 1.0 collective-permute-done.5
  40.5 0.7 fusion.1
  42.1 6.1 %collective-permute-start.8 = (f32[3,1,7,7,128]{4,1,3,2,0:T(1,128)S(1)}, f32[3,1,7,7,128]{4,1,3,2,0:T(1,128)S(1)}, u32[]{:S(2)}, u32[]{:S(2)}) collective-permute-start(f32[3,1,7,7,128]{4,1,3,2,0:T(1,128)S(1)} %slice.347), channel_id=1, source_target_pairs={{0,248},{8,0},{16,8},{24,16},{32,24},{40,32},{48,40},{56,48},{64,5... | collective-permute-start | bytes 225800 | tf_op jit(solution)/shard_map/ppermute | solution.py:15
  48.2 1.3 collective-permute-start.10
  49.6 0.7 fusion.8
  51.6 2.1 collective-permute-done.10
  53.7 0.7 fusion.10
  54.4 0.7 fusion.55
  55.5 4.1 %collective-permute-start.11 = (f32[3,7,1,7,128]{4,1,3,2,0:T(8,128)S(1)}, f32[3,7,1,7,128]{4,1,3,2,0:T(8,128)S(1)}, u32[]{:S(2)}, u32[]{:S(2)}) collective-permute-start(f32[3,7,1,7,128]{4,1,3,2,0:T(8,128)S(1)} %pad_add_fusion.9), channel_id=1, source_target_pairs={{0,1},{1,2},{2,3},{3,4},{4,5},{5,6},{6,7},{8,9},{9,10},{10,11},{11... | collective-permute-start | bytes 225800 | tf_op jit(solution)/shard_map/ppermute | solution.py:21
  59.7 1.0 collective-permute-done.9
  61.7 84.8 %all-reduce.24 = (f32[3]{0:T(128)S(1)}, f32[3]{0:T(128)S(1)}) all-reduce(f32[3]{0:T(128)S(1)} %get-tuple-element.11, f32[3]{0:T(128)S(1)} %get-tuple-element.10), channel_id=1, replica_groups=mesh['px'=32,'py'=8] {'px','py'}, use_global_device_ids=true, to_apply=%region_2.3 | all-reduce | flops 6 | bytes 48 | tf_op jit(solution)/shard_map/psum | solution.py:200
  146.8 74.6 %psum.37 = f32[3]{0:T(128)S(1)} all-reduce(f32[3]{0:T(128)S(1)} %get-tuple-element.16), channel_id=1, replica_groups=mesh['px'=32,'py'=8] {'px','py'}, use_global_device_ids=true, to_apply=%region_6.7 | all-reduce | flops 3 | bytes 24 | tf_op jit(solution)/shard_map/psum | solution.py:200
  221.9 0.8 copy-done.2
  222.7 0.7 fusion
  224.3 0.8 collective-permute-start.12
  225.0 1.3 collective-permute-start.14
  226.5 1.7 collective-permute-done.12
  228.1 0.7 fusion.12
  230.3 0.9 copy-done.4
  231.2 0.7 fusion.14
  231.9 0.7 fusion.57
  232.7 2.3 collective-permute-start.13
  235.1 1.8 collective-permute-start.15
  237.2 1.7 collective-permute-done.15
  239.4 78.2 %psum.38 = f32[3]{0:T(128)S(1)} all-reduce(f32[3]{0:T(128)S(1)} %get-tuple-element.14), channel_id=1, replica_groups=mesh['px'=32,'py'=8] {'px','py'}, use_global_device_ids=true, to_apply=%region_8.9 | all-reduce | flops 3 | bytes 24 | tf_op jit(solution)/shard_map/psum | solution.py:236
  317.9 73.5 %psum.39 = f32[3]{0:T(128)S(1)} all-reduce(f32[3]{0:T(128)S(1)} %multiply_reduce_fusion), channel_id=1, replica_groups=mesh['px'=32,'py'=8] {'px','py'}, use_global_device_ids=true, to_apply=%region_10.11 | all-reduce | flops 3 | bytes 24 | tf_op jit(solution)/shard_map/psum | solution.py:200
  391.8 0.9 copy.203
  392.8 0.9 copy.204
  (161 shorter events, 16.2 us)
Async XLA Ops:
  0.6 1.1 copy-start.11
  1.9 17.1 %collective-permute-start.4 = (f32[7,1,7,128]{3,0,2,1:T(8,128)S(1)}, f32[7,1,7,128]{3,0,2,1:T(8,128)}, u32[]{:S(2)}, u32[]{:S(2)}) collective-permute-start(f32[7,1,7,128]{3,0,2,1:T(8,128)S(1)} %slice.328), channel_id=1, source_target_pairs={{1,0},{2,1},{3,2},{4,3},{5,4},{6,5},{7,6},{9,8},{10,9},{11,10},{12... | collective-permute-start | bytes 75272 | tf_op jit(solution)/shard_map/ppermute | solution.py:21
  3.8 3.2 slice-start
  3.8 21.4 %collective-permute-start.1 = (f32[1,7,7,128]{3,0,2,1:T(1,128)}, f32[1,7,7,128]{3,0,2,1:T(1,128)}, u32[]{:S(2)}, u32[]{:S(2)}) collective-permute-start(f32[1,7,7,128]{3,0,2,1:T(1,128)} %slice.324), channel_id=1, source_target_pairs={{0,248},{8,0},{16,8},{24,16},{32,24},{40,32},{48,40},{56,48},{64,5... | collective-permute-start | bytes 75272 | tf_op jit(solution)/shard_map/ppermute | solution.py:15
  7.7 2.9 slice-start.1
  7.7 20.9 %collective-permute-start = (f32[3,1,7,7,128]{4,1,3,2,0:T(1,128)}, f32[3,1,7,7,128]{4,1,3,2,0:T(1,128)}, u32[]{:S(2)}, u32[]{:S(2)}) collective-permute-start(f32[3,1,7,7,128]{4,1,3,2,0:T(1,128)} %copy.257), channel_id=1, source_target_pairs={{0,248},{8,0},{16,8},{24,16},{32,24},{40,32},{48,40},{56,48},{64,5... | collective-permute-start | bytes 225800 | tf_op jit(solution)/shard_map/ppermute | solution.py:15
  11.3 21.5 %collective-permute-start.3 = (f32[3,7,1,7,128]{4,2,3,1,0:T(1,128)}, f32[3,7,1,7,128]{4,2,3,1,0:T(1,128)S(1)}, u32[]{:S(2)}, u32[]{:S(2)}) collective-permute-start(f32[3,7,1,7,128]{4,2,3,1,0:T(1,128)} %copy.258), channel_id=1, source_target_pairs={{1,0},{2,1},{3,2},{4,3},{5,4},{6,5},{7,6},{9,8},{10,9},{11,10},{12... | collective-permute-start | bytes 225800 | tf_op jit(solution)/shard_map/ppermute | solution.py:21
  12.7 0.7 copy-start.12
  13.4 0.7 copy-start.10
  13.5 1.1 copy-start
  14.0 26.4 %copy-start.1 = (f32[7,7,8,128]{3,2,1,0:T(8,128)}, f32[7,7,8,128]{3,2,1,0:T(8,128)S(1)}, u32[]{:S(2)}) copy-start(f32[7,7,8,128]{3,2,1,0:T(8,128)S(1)} %copy.176) | copy-start | bytes 602116
  15.0 0.7 copy-start.7
  17.4 0.9 copy-start.8
  18.9 42.2 %copy-start.5 = (f32[7,7,7,128]{3,0,2,1:T(8,128)}, f32[7,7,7,128]{3,0,2,1:T(8,128)S(1)}, u32[]{:S(2)}) copy-start(f32[7,7,7,128]{3,0,2,1:T(8,128)S(1)} %copy.162) | copy-start | bytes 526852
  19.9 33.9 %copy-start.3 = (f32[7,8,7,128]{3,1,2,0:T(8,128)}, f32[7,8,7,128]{3,1,2,0:T(8,128)S(1)}, u32[]{:S(2)}) copy-start(f32[7,8,7,128]{3,1,2,0:T(8,128)S(1)} %copy.170) | copy-start | bytes 602116
  20.3 6.2 %collective-permute-start.7 = (f32[7,1,7,128]{3,0,2,1:T(8,128)S(1)}, f32[7,1,7,128]{3,0,2,1:T(8,128)S(1)}, u32[]{:S(2)}, u32[]{:S(2)}) collective-permute-start(f32[7,1,7,128]{3,0,2,1:T(8,128)S(1)} %pad_add_fusion.14), channel_id=1, source_target_pairs={{0,1},{1,2},{2,3},{3,4},{4,5},{5,6},{6,7},{8,9},{9,10},{10,11},{11... | collective-permute-start | bytes 75272 | tf_op jit(solution)/shard_map/ppermute | solution.py:21
  26.5 1.9 collective-permute-start.6
  31.2 7.1 %collective-permute-start.2 = (f32[3,1,7,7,128]{4,1,3,2,0:T(1,128)S(1)}, f32[3,1,7,7,128]{4,1,3,2,0:T(1,128)S(1)}, u32[]{:S(2)}, u32[]{:S(2)}) collective-permute-start(f32[3,1,7,7,128]{4,1,3,2,0:T(1,128)S(1)} %pad_add_fusion.13), channel_id=1, source_target_pairs={{0,8},{8,16},{16,24},{24,32},{32,40},{40,48},{48,56},{56,64},{64,7... | collective-permute-start | bytes 225800 | tf_op jit(solution)/shard_map/ppermute | solution.py:15
  34.5 5.1 %collective-permute-start.5 = (f32[3,7,1,7,128]{4,1,3,2,0:T(8,128)S(1)}, f32[3,7,1,7,128]{4,1,3,2,0:T(8,128)S(1)}, u32[]{:S(2)}, u32[]{:S(2)}) collective-permute-start(f32[3,7,1,7,128]{4,1,3,2,0:T(8,128)S(1)} %pad_add_fusion.10), channel_id=1, source_target_pairs={{0,1},{1,2},{2,3},{3,4},{4,5},{5,6},{6,7},{8,9},{9,10},{10,11},{11... | collective-permute-start | bytes 225800 | tf_op jit(solution)/shard_map/ppermute | solution.py:21
  38.5 1.1 copy-start.9
  42.1 7.5 %collective-permute-start.8 = (f32[3,1,7,7,128]{4,1,3,2,0:T(1,128)S(1)}, f32[3,1,7,7,128]{4,1,3,2,0:T(1,128)S(1)}, u32[]{:S(2)}, u32[]{:S(2)}) collective-permute-start(f32[3,1,7,7,128]{4,1,3,2,0:T(1,128)S(1)} %slice.347), channel_id=1, source_target_pairs={{0,248},{8,0},{16,8},{24,16},{32,24},{40,32},{48,40},{56,48},{64,5... | collective-permute-start | bytes 225800 | tf_op jit(solution)/shard_map/ppermute | solution.py:15
  48.2 5.5 %collective-permute-start.10 = (f32[3,7,1,7,128]{4,1,3,2,0:T(8,128)S(1)}, f32[3,7,1,7,128]{4,1,3,2,0:T(8,128)S(1)}, u32[]{:S(2)}, u32[]{:S(2)}) collective-permute-start(f32[3,7,1,7,128]{4,1,3,2,0:T(8,128)S(1)} %slice.350), channel_id=1, source_target_pairs={{1,0},{2,1},{3,2},{4,3},{5,4},{6,5},{7,6},{9,8},{10,9},{11,10},{12... | collective-permute-start | bytes 225800 | tf_op jit(solution)/shard_map/ppermute | solution.py:21
  55.3 5.4 %collective-permute-start.9 = (f32[3,1,7,7,128]{4,1,3,2,0:T(1,128)S(1)}, f32[3,1,7,7,128]{4,1,3,2,0:T(1,128)S(1)}, u32[]{:S(2)}, u32[]{:S(2)}) collective-permute-start(f32[3,1,7,7,128]{4,1,3,2,0:T(1,128)S(1)} %pad_add_fusion.12), channel_id=1, source_target_pairs={{0,8},{8,16},{16,24},{24,32},{32,40},{40,48},{48,56},{56,64},{64,7... | collective-permute-start | bytes 225800 | tf_op jit(solution)/shard_map/ppermute | solution.py:15
  55.5 5.6 %collective-permute-start.11 = (f32[3,7,1,7,128]{4,1,3,2,0:T(8,128)S(1)}, f32[3,7,1,7,128]{4,1,3,2,0:T(8,128)S(1)}, u32[]{:S(2)}, u32[]{:S(2)}) collective-permute-start(f32[3,7,1,7,128]{4,1,3,2,0:T(8,128)S(1)} %pad_add_fusion.9), channel_id=1, source_target_pairs={{0,1},{1,2},{2,3},{3,4},{4,5},{5,6},{6,7},{8,9},{9,10},{10,11},{11... | collective-permute-start | bytes 225800 | tf_op jit(solution)/shard_map/ppermute | solution.py:21
  221.7 0.9 copy-start.2
  224.3 3.9 collective-permute-start.12
  225.0 5.2 %collective-permute-start.14 = (f32[3,7,1,7,128]{4,1,3,2,0:T(8,128)S(1)}, f32[3,7,1,7,128]{4,1,3,2,0:T(8,128)S(1)}, u32[]{:S(2)}, u32[]{:S(2)}) collective-permute-start(f32[3,7,1,7,128]{4,1,3,2,0:T(8,128)S(1)} %slice.362), channel_id=1, source_target_pairs={{1,0},{2,1},{3,2},{4,3},{5,4},{6,5},{7,6},{9,8},{10,9},{11,10},{12... | collective-permute-start | bytes 225800 | tf_op jit(solution)/shard_map/ppermute | solution.py:21
  230.2 0.9 copy-start.4
  232.7 4.3 %collective-permute-start.13 = (f32[3,1,7,7,128]{4,1,3,2,0:T(1,128)S(1)}, f32[3,1,7,7,128]{4,1,3,2,0:T(1,128)S(1)}, u32[]{:S(2)}, u32[]{:S(2)}) collective-permute-start(f32[3,1,7,7,128]{4,1,3,2,0:T(1,128)S(1)} %pad_add_fusion.11), channel_id=1, source_target_pairs={{0,8},{8,16},{16,24},{24,32},{32,40},{40,48},{48,56},{56,64},{64,7... | collective-permute-start | bytes 225800 | tf_op jit(solution)/shard_map/ppermute | solution.py:15
  235.1 3.8 collective-permute-start.15
  237.2 1.7 copy-start.6
where the time goes:
time: 395 us; the launch traced here: 394 us
  blocking collectives  311 us (79%)
  starting transfers between devices  36.5 us (9%)
  matrix products  14.2 us (4%)
  local copies, waits for them, and re-layouts  11.6 us (3%)
  waiting for transfers between devices  9.8 us (2%)
  other arithmetic  8.82 us (2%)
    psum x3, blocking collectives, energy_sum(): lax.psum(jnp.sum(residual * precond, axis=(1, 2, 3, 4)), ('px', 'py'))  233 us
    psum x1, blocking collectives, body(): lax.psum(jnp.sum(direction * applied, axis=(1, 2, 3, 4)), ('px', 'py'))  78.2 us
    ppermute x8, starting transfers between devices, passed_along(): return lax.ppermute(block, axis, route)  19.6 us
    ppermute x8, starting transfers between devices, shifted(): lax.ppermute(value, axis, [(i, (i + by) % count) for i in range(count)])  16.9 us
  transfers between devices with their start and end apart: 16, of which 8 were waited for; matrix products, arithmetic and copies ran while one was open for 5% of the time, Pallas kernels for 0%

commit v1 on v0

--- a/solution.py
+++ b/solution.py
@@ -233,7 +233,7 @@
     direction = precond
     for iteration in range(ITERS):
         applied = operate(direction)
-        curvature = lax.psum(jnp.sum(direction * applied, axis=(1, 2, 3, 4)), ("px", "py"))
+        curvature = lax.psum(lax.psum(jnp.sum(direction * applied, axis=(1, 2, 3, 4)), "px"), "py")
         step_length = spread(energy_now / curvature)
         solution = solution + step_length * direction
         residual = residual - step_length * applied

time: 395 us -> 477 us (1.21)
  blocking collectives: 311 us -> 392 us
    psum x1 -> x4, blocking collectives: 78.2 us -> 162 us  [the longest x2 133 us: body(): lax.psum(jnp.sum(direction * applied, axis=(1, 2, 3, 4)), 'px')]
  transfers between devices with their start and end apart: 16 -> 16, of which waited for: 8 -> 8; matrix products, arithmetic and copies ran while one was open for 5% -> 4% of each run, Pallas kernels for 0% -> 0%
where the time goes in v1:
time: 477 us; the launch traced here: 476 us
  blocking collectives  392 us (82%)
  starting transfers between devices  38.4 us (8%)
  matrix products  14.2 us (3%)
  local copies, waits for them, and re-layouts  11.6 us (2%)
  waiting for transfers between devices  9.69 us (2%)
  other arithmetic  8.82 us (2%)
    psum x3, blocking collectives, energy_sum(): lax.psum(jnp.sum(residual * precond, axis=(1, 2, 3, 4)), ('px', 'py'))  230 us
    psum x2, blocking collectives, body(): lax.psum(jnp.sum(direction * applied, axis=(1, 2, 3, 4)), 'px')  133 us
    psum x2, blocking collectives, body(): lax.psum(lax.psum(jnp.sum(direction * applied, axis=(1, 2, 3, 4)), 'px'),...  28.5 us
    ppermute x8, starting transfers between devices, passed_along(): return lax.ppermute(block, axis, route)  21.1 us
    ppermute x8, starting transfers between devices, shifted(): lax.ppermute(value, axis, [(i, (i + by) % count) for i in range(count)])  17.3 us
  transfers between devices with their start and end apart: 16, of which 8 were waited for; matrix products, arithmetic and copies ran while one was open for 4% of the time, Pallas kernels for 0%

profile of v1, /device:TPU:1, one launch (start us, length us, event | category | flops | bytes accessed | tf_op | source)
XLA Modules:
  0.0 476.5 jit_solution(13043440396178364491)
XLA Ops:
  0.6 1.1 multiply_reduce_fusion.5
  1.9 1.3 collective-permute-start.4
  3.8 3.2 collective-permute-start.1
  7.0 0.7 copy.257
  7.7 2.9 collective-permute-start
  10.6 0.7 copy.258
  11.4 1.3 collective-permute-start.3
  15.7 0.7 fusion.2
  17.7 0.7 copy-done.8
  19.0 0.9 maximum_multiply_fusion
  20.4 4.8 %collective-permute-start.7 = (f32[7,1,7,128]{3,0,2,1:T(8,128)S(1)}, f32[7,1,7,128]{3,0,2,1:T(8,128)S(1)}, u32[]{:S(2)}, u32[]{:S(2)}) collective-permute-start(f32[7,1,7,128]{3,0,2,1:T(8,128)S(1)} %pad_add_fusion.14), channel_id=1, source_target_pairs={{0,1},{1,2},{2,3},{3,4},{4,5},{5,6},{6,7},{8,9},{9,10},{10,11},{11... | collective-permute-start | bytes 75272 | tf_op jit(solution)/shard_map/ppermute | solution.py:21
  25.2 0.8 maximum_multiply_fusion.2
  26.6 1.8 collective-permute-done.6
  28.6 1.6 fusion.4
  31.3 1.5 collective-permute-start.2
  32.9 0.7 fusion.6
  34.5 3.7 collective-permute-start.5
  38.6 1.0 collective-permute-done.5
  40.5 0.7 fusion.1
  42.1 6.0 %collective-permute-start.8 = (f32[3,1,7,7,128]{4,1,3,2,0:T(1,128)S(1)}, f32[3,1,7,7,128]{4,1,3,2,0:T(1,128)S(1)}, u32[]{:S(2)}, u32[]{:S(2)}) collective-permute-start(f32[3,1,7,7,128]{4,1,3,2,0:T(1,128)S(1)} %slice.347), channel_id=1, source_target_pairs={{0,248},{8,0},{16,8},{24,16},{32,24},{40,32},{48,40},{56,48},{64,5... | collective-permute-start | bytes 225800 | tf_op jit(solution)/shard_map/ppermute | solution.py:15
  48.2 1.3 collective-permute-start.10
  49.6 0.7 fusion.8
  51.6 2.1 collective-permute-done.10
  53.8 0.7 fusion.10
  54.5 0.7 fusion.55
  55.5 4.1 collective-permute-start.11
  59.7 1.0 collective-permute-done.9
  61.7 68.2 %psum.50 = f32[3]{0:T(128)S(1)} all-reduce(f32[3]{0:T(128)S(1)} %get-tuple-element.10), channel_id=1, replica_groups=mesh['px'=32,'py'=8] {'px'}, use_global_device_ids=true, to_apply=%region_4.5 | all-reduce | flops 3 | bytes 24 | tf_op jit(solution)/shard_map/psum | solution.py:236
  129.9 16.2 %psum.51 = f32[3]{0:T(128)S(1)} all-reduce(f32[3]{0:T(128)S(1)} %psum.50), channel_id=1, replica_groups=mesh['px'=32,'py'=8] {'py'}, use_global_device_ids=true, to_apply=%region_5.6 | all-reduce | flops 3 | bytes 24 | tf_op jit(solution)/shard_map/psum | solution.py:236
  146.1 79.0 %psum.49 = f32[3]{0:T(128)S(1)} all-reduce(f32[3]{0:T(128)S(1)} %get-tuple-element.11), channel_id=1, replica_groups=mesh['px'=32,'py'=8] {'px','py'}, use_global_device_ids=true, to_apply=%region_2.3 | all-reduce | flops 3 | bytes 24 | tf_op jit(solution)/shard_map/psum | solution.py:200
  225.5 73.9 %psum.52 = f32[3]{0:T(128)S(1)} all-reduce(f32[3]{0:T(128)S(1)} %get-tuple-element.14), channel_id=1, replica_groups=mesh['px'=32,'py'=8] {'px','py'}, use_global_device_ids=true, to_apply=%region_7.8 | all-reduce | flops 3 | bytes 24 | tf_op jit(solution)/shard_map/psum | solution.py:200
  299.8 0.8 copy-done.2
  300.6 0.7 fusion
  302.2 0.8 collective-permute-start.12
  303.0 1.3 collective-permute-start.14
  304.4 1.7 collective-permute-done.12
  306.1 0.7 fusion.12
  308.4 0.9 copy-done.4
  309.3 0.7 fusion.14
  310.0 0.7 fusion.57
  310.9 2.7 collective-permute-start.13
  313.6 3.4 collective-permute-start.15
  317.3 1.4 collective-permute-done.15
  319.2 65.0 %psum.53 = f32[3]{0:T(128)S(1)} all-reduce(f32[3]{0:T(128)S(1)} %get-tuple-element.12), channel_id=1, replica_groups=mesh['px'=32,'py'=8] {'px'}, use_global_device_ids=true, to_apply=%region_9.10 | all-reduce | flops 3 | bytes 24 | tf_op jit(solution)/shard_map/psum | solution.py:236
  384.2 12.3 %psum.54 = f32[3]{0:T(128)S(1)} all-reduce(f32[3]{0:T(128)S(1)} %psum.53), channel_id=1, replica_groups=mesh['px'=32,'py'=8] {'py'}, use_global_device_ids=true, to_apply=%region_10.11 | all-reduce | flops 3 | bytes 24 | tf_op jit(solution)/shard_map/psum | solution.py:236
  396.8 77.4 %psum.55 = f32[3]{0:T(128)S(1)} all-reduce(f32[3]{0:T(128)S(1)} %multiply_reduce_fusion), channel_id=1, replica_groups=mesh['px'=32,'py'=8] {'px','py'}, use_global_device_ids=true, to_apply=%region_12.13 | all-reduce | flops 3 | bytes 24 | tf_op jit(solution)/shard_map/psum | solution.py:200
  474.6 0.9 copy.203
  475.5 0.9 copy.204
  (164 shorter events, 18.5 us)
Async XLA Ops:
  0.6 1.1 copy-start.11
  1.9 17.1 %collective-permute-start.4 = (f32[7,1,7,128]{3,0,2,1:T(8,128)S(1)}, f32[7,1,7,128]{3,0,2,1:T(8,128)}, u32[]{:S(2)}, u32[]{:S(2)}) collective-permute-start(f32[7,1,7,128]{3,0,2,1:T(8,128)S(1)} %slice.328), channel_id=1, source_target_pairs={{1,0},{2,1},{3,2},{4,3},{5,4},{6,5},{7,6},{9,8},{10,9},{11,10},{12... | collective-permute-start | bytes 75272 | tf_op jit(solution)/shard_map/ppermute | solution.py:21
  3.8 3.2 slice-start
  3.8 21.4 %collective-permute-start.1 = (f32[1,7,7,128]{3,0,2,1:T(1,128)}, f32[1,7,7,128]{3,0,2,1:T(1,128)}, u32[]{:S(2)}, u32[]{:S(2)}) collective-permute-start(f32[1,7,7,128]{3,0,2,1:T(1,128)} %slice.324), channel_id=1, source_target_pairs={{0,248},{8,0},{16,8},{24,16},{32,24},{40,32},{48,40},{56,48},{64,5... | collective-permute-start | bytes 75272 | tf_op jit(solution)/shard_map/ppermute | solution.py:15
  7.7 2.9 slice-start.1
  7.7 20.9 %collective-permute-start = (f32[3,1,7,7,128]{4,1,3,2,0:T(1,128)}, f32[3,1,7,7,128]{4,1,3,2,0:T(1,128)}, u32[]{:S(2)}, u32[]{:S(2)}) collective-permute-start(f32[3,1,7,7,128]{4,1,3,2,0:T(1,128)} %copy.257), channel_id=1, source_target_pairs={{0,248},{8,0},{16,8},{24,16},{32,24},{40,32},{48,40},{56,48},{64,5... | collective-permute-start | bytes 225800 | tf_op jit(solution)/shard_map/ppermute | solution.py:15
  11.4 21.5 %collective-permute-start.3 = (f32[3,7,1,7,128]{4,2,3,1,0:T(1,128)}, f32[3,7,1,7,128]{4,2,3,1,0:T(1,128)S(1)}, u32[]{:S(2)}, u32[]{:S(2)}) collective-permute-start(f32[3,7,1,7,128]{4,2,3,1,0:T(1,128)} %copy.258), channel_id=1, source_target_pairs={{1,0},{2,1},{3,2},{4,3},{5,4},{6,5},{7,6},{9,8},{10,9},{11,10},{12... | collective-permute-start | bytes 225800 | tf_op jit(solution)/shard_map/ppermute | solution.py:21
  12.7 0.7 copy-start.12
  13.4 0.7 copy-start.10
  13.5 1.1 copy-start
  14.1 26.4 %copy-start.1 = (f32[7,7,8,128]{3,2,1,0:T(8,128)}, f32[7,7,8,128]{3,2,1,0:T(8,128)S(1)}, u32[]{:S(2)}) copy-start(f32[7,7,8,128]{3,2,1,0:T(8,128)S(1)} %copy.176) | copy-start | bytes 602116
  15.0 0.7 copy-start.7
  17.4 0.9 copy-start.8
  18.9 42.2 %copy-start.5 = (f32[7,7,7,128]{3,0,2,1:T(8,128)}, f32[7,7,7,128]{3,0,2,1:T(8,128)S(1)}, u32[]{:S(2)}) copy-start(f32[7,7,7,128]{3,0,2,1:T(8,128)S(1)} %copy.162) | copy-start | bytes 526852
  19.9 33.9 %copy-start.3 = (f32[7,8,7,128]{3,1,2,0:T(8,128)}, f32[7,8,7,128]{3,1,2,0:T(8,128)S(1)}, u32[]{:S(2)}) copy-start(f32[7,8,7,128]{3,1,2,0:T(8,128)S(1)} %copy.170) | copy-start | bytes 602116
  20.4 6.2 %collective-permute-start.7 = (f32[7,1,7,128]{3,0,2,1:T(8,128)S(1)}, f32[7,1,7,128]{3,0,2,1:T(8,128)S(1)}, u32[]{:S(2)}, u32[]{:S(2)}) collective-permute-start(f32[7,1,7,128]{3,0,2,1:T(8,128)S(1)} %pad_add_fusion.14), channel_id=1, source_target_pairs={{0,1},{1,2},{2,3},{3,4},{4,5},{5,6},{6,7},{8,9},{9,10},{10,11},{11... | collective-permute-start | bytes 75272 | tf_op jit(solution)/shard_map/ppermute | solution.py:21
  26.5 1.9 collective-permute-start.6
  31.3 7.1 %collective-permute-start.2 = (f32[3,1,7,7,128]{4,1,3,2,0:T(1,128)S(1)}, f32[3,1,7,7,128]{4,1,3,2,0:T(1,128)S(1)}, u32[]{:S(2)}, u32[]{:S(2)}) collective-permute-start(f32[3,1,7,7,128]{4,1,3,2,0:T(1,128)S(1)} %pad_add_fusion.13), channel_id=1, source_target_pairs={{0,8},{8,16},{16,24},{24,32},{32,40},{40,48},{48,56},{56,64},{64,7... | collective-permute-start | bytes 225800 | tf_op jit(solution)/shard_map/ppermute | solution.py:15
  34.5 5.1 %collective-permute-start.5 = (f32[3,7,1,7,128]{4,1,3,2,0:T(8,128)S(1)}, f32[3,7,1,7,128]{4,1,3,2,0:T(8,128)S(1)}, u32[]{:S(2)}, u32[]{:S(2)}) collective-permute-start(f32[3,7,1,7,128]{4,1,3,2,0:T(8,128)S(1)} %pad_add_fusion.10), channel_id=1, source_target_pairs={{0,1},{1,2},{2,3},{3,4},{4,5},{5,6},{6,7},{8,9},{9,10},{10,11},{11... | collective-permute-start | bytes 225800 | tf_op jit(solution)/shard_map/ppermute | solution.py:21
  38.6 1.1 copy-start.9
  42.1 7.5 %collective-permute-start.8 = (f32[3,1,7,7,128]{4,1,3,2,0:T(1,128)S(1)}, f32[3,1,7,7,128]{4,1,3,2,0:T(1,128)S(1)}, u32[]{:S(2)}, u32[]{:S(2)}) collective-permute-start(f32[3,1,7,7,128]{4,1,3,2,0:T(1,128)S(1)} %slice.347), channel_id=1, source_target_pairs={{0,248},{8,0},{16,8},{24,16},{32,24},{40,32},{48,40},{56,48},{64,5... | collective-permute-start | bytes 225800 | tf_op jit(solution)/shard_map/ppermute | solution.py:15
  48.2 5.5 %collective-permute-start.10 = (f32[3,7,1,7,128]{4,1,3,2,0:T(8,128)S(1)}, f32[3,7,1,7,128]{4,1,3,2,0:T(8,128)S(1)}, u32[]{:S(2)}, u32[]{:S(2)}) collective-permute-start(f32[3,7,1,7,128]{4,1,3,2,0:T(8,128)S(1)} %slice.350), channel_id=1, source_target_pairs={{1,0},{2,1},{3,2},{4,3},{5,4},{6,5},{7,6},{9,8},{10,9},{11,10},{12... | collective-permute-start | bytes 225800 | tf_op jit(solution)/shard_map/ppermute | solution.py:21
  55.4 5.4 %collective-permute-start.9 = (f32[3,1,7,7,128]{4,1,3,2,0:T(1,128)S(1)}, f32[3,1,7,7,128]{4,1,3,2,0:T(1,128)S(1)}, u32[]{:S(2)}, u32[]{:S(2)}) collective-permute-start(f32[3,1,7,7,128]{4,1,3,2,0:T(1,128)S(1)} %pad_add_fusion.12), channel_id=1, source_target_pairs={{0,8},{8,16},{16,24},{24,32},{32,40},{40,48},{48,56},{56,64},{64,7... | collective-permute-start | bytes 225800 | tf_op jit(solution)/shard_map/ppermute | solution.py:15
  55.5 5.6 %collective-permute-start.11 = (f32[3,7,1,7,128]{4,1,3,2,0:T(8,128)S(1)}, f32[3,7,1,7,128]{4,1,3,2,0:T(8,128)S(1)}, u32[]{:S(2)}, u32[]{:S(2)}) collective-permute-start(f32[3,7,1,7,128]{4,1,3,2,0:T(8,128)S(1)} %pad_add_fusion.9), channel_id=1, source_target_pairs={{0,1},{1,2},{2,3},{3,4},{4,5},{5,6},{6,7},{8,9},{9,10},{10,11},{11... | collective-permute-start | bytes 225800 | tf_op jit(solution)/shard_map/ppermute | solution.py:21
  299.7 0.9 copy-start.2
  302.2 3.9 collective-permute-start.12
  303.0 5.4 %collective-permute-start.14 = (f32[3,7,1,7,128]{4,1,3,2,0:T(8,128)S(1)}, f32[3,7,1,7,128]{4,1,3,2,0:T(8,128)S(1)}, u32[]{:S(2)}, u32[]{:S(2)}) collective-permute-start(f32[3,7,1,7,128]{4,1,3,2,0:T(8,128)S(1)} %slice.362), channel_id=1, source_target_pairs={{1,0},{2,1},{3,2},{4,3},{5,4},{6,5},{7,6},{9,8},{10,9},{11,10},{12... | collective-permute-start | bytes 225800 | tf_op jit(solution)/shard_map/ppermute | solution.py:21
  308.4 0.9 copy-start.4
  310.9 6.2 %collective-permute-start.13 = (f32[3,1,7,7,128]{4,1,3,2,0:T(1,128)S(1)}, f32[3,1,7,7,128]{4,1,3,2,0:T(1,128)S(1)}, u32[]{:S(2)}, u32[]{:S(2)}) collective-permute-start(f32[3,1,7,7,128]{4,1,3,2,0:T(1,128)S(1)} %pad_add_fusion.11), channel_id=1, source_target_pairs={{0,8},{8,16},{16,24},{24,32},{32,40},{40,48},{48,56},{56,64},{64,7... | collective-permute-start | bytes 225800 | tf_op jit(solution)/shard_map/ppermute | solution.py:15
  313.6 5.1 %collective-permute-start.15 = (f32[3,7,1,7,128]{4,1,3,2,0:T(8,128)S(1)}, f32[3,7,1,7,128]{4,1,3,2,0:T(8,128)S(1)}, u32[]{:S(2)}, u32[]{:S(2)}) collective-permute-start(f32[3,7,1,7,128]{4,1,3,2,0:T(8,128)S(1)} %pad_add_fusion.8), channel_id=1, source_target_pairs={{0,1},{1,2},{2,3},{3,4},{4,5},{5,6},{6,7},{8,9},{9,10},{10,11},{11... | collective-permute-start | bytes 225800 | tf_op jit(solution)/shard_map/ppermute | solution.py:21
  317.3 1.5 copy-start.6
